TPU v7x, 128 devices: a whole 4x4x4 slice. The times are simulated.
128 devices in a mesh: gy: 8 (over z, y_lo), gx: 16 (over x, y_hi, core).
Axes of the slice: x: 4, y: 4 (y_hi: 2, y_lo: 2; y = y_hi * 2 + y_lo), z: 4, core: 2. Of those that a mesh axis runs over, the one named last changes fastest.
Arguments:
- radar_input: bfloat16 [512, 1024, 256], P('gy', 'gx'), may hold values from -6 to 6
- conv_weight: bfloat16 [3, 3, 256, 256], replicated, may hold values from -0.125 to 0.125
- conv_bias: float32 [256], replicated, may hold values from -3 to 3
- row_gain: float32 [256], replicated, may hold values from 0.1 to 1.9
- row_qkv: bfloat16 [256, 768], replicated, may hold values from -8 to 8
- row_out: bfloat16 [256, 256], replicated, may hold values from -0.375 to 0.375
- col_gain: float32 [256], replicated, may hold values from 0.1 to 1.9
- col_qkv: bfloat16 [256, 768], replicated, may hold values from -8 to 8
- col_out: bfloat16 [256, 256], replicated, may hold values from -0.375 to 0.375
Outputs:
- block_output: bfloat16 [512, 1024, 256], P('gy', 'gx')
All inputs are finite; a program needn't handle non-finite values.
Results may differ from a plain program's by a relative error of at most 0.012.
Values may be sent and summed in bfloat16 or wider, within the bound.
No kernel may reach another device: no remote copies, remote signals or barrier semaphores. Data moves between devices by JAX's collectives and lax.ppermute only.
A program may use at most 128 MiB of HBM per device.

v0:
```python
import functools

import jax
import jax.numpy as jnp
from jax import lax
from jax.experimental import pallas as pl
from jax.experimental.pallas import tpu as pltpu
from jax.sharding import PartitionSpec as P

HEADS = 8
WIDTH = 32
C = 256
SCORE_SCALE = 1.4426950408889634 / 32**0.5
SAFE_SQUARE = 62.0**2
STARTED = WIDTH + 8
VMEM_LIMIT = 56 * 2**20
F32 = jnp.float32
BF16 = jnp.bfloat16


def dot(a, b):
    return jnp.dot(a, b, preferred_element_type=F32)


def dot_nt(a, b):
    return lax.dot_general(a, b, (((1,), (1,)), ((), ())), preferred_element_type=F32)


def dot_tn(a, b):
    return lax.dot_general(a, b, (((0,), (0,)), ((), ())), preferred_element_type=F32)


def normalize(values, gain):
    center = jnp.mean(values, axis=-1, keepdims=True)
    shifted = values - center
    spread = jnp.mean(shifted * shifted, axis=-1, keepdims=True)
    return (shifted * lax.rsqrt(spread + 1e-05) * gain).astype(BF16)


def project(normed, wq_t, wk, wv_t):
    keys = dot(normed, wk)
    queries = dot_nt(wq_t, normed) * SCORE_SCALE
    values = dot_nt(wv_t, normed)
    q_norms = jnp.sum((queries * queries).reshape(HEADS, WIDTH, normed.shape[0]), axis=1)
    head_of = lax.broadcasted_iota(jnp.int32, (C, 128), 0) // WIDTH
    column = lax.broadcasted_iota(jnp.int32, (C, 128), 1)
    pick = jnp.where(head_of == column, 1.0, 0.0).astype(BF16)
    k_norms = dot((keys * keys).astype(BF16), pick)
    rounded = keys.astype(BF16), queries.astype(BF16), values.astype(BF16)
    return rounded, jnp.max(q_norms), jnp.max(k_norms)


def attend(
    safe, sources, qt_ref, att_ref, count, tile, part, joined, started=None, unfinished=False
):
    length = qt_ref.shape[1] // count

    def channels(head, heads=1):
        return slice(head * WIDTH, (head + heads) * WIDTH)

    def with_ones(vt_ref, head, cells, size, heads=1):
        ones = jnp.ones((16, size), BF16)
        return jnp.concatenate([vt_ref[channels(head, heads), cells], ones], axis=0)

    def fast():
        units = [
            (sequence, start, head)
            for sequence in range(count)
            for start in range(0, length, tile)
            for head in range(0, HEADS, joined)
        ]
        pieces = [
            (k_ref, vt_ref, k_ref.shape[0] // count, start)
            for k_ref, vt_ref in (sources if started is None else sources[-1:])
            for start in range(0, k_ref.shape[0] // count, part)
        ]
        zeros = jnp.zeros((WIDTH, tile), BF16)

        def diagonal(unit):
            sequence, start, head = unit
            base = sequence * length + start
            rows = []
            for own in range(joined):
                queries = qt_ref[channels(head + own), base : base + tile]
                row = [queries if own == other else zeros for other in range(joined)]
                rows.append(jnp.concatenate(row, axis=1))
            return jnp.concatenate(rows, axis=0)

        def weigh(unit, queries, piece):
            sequence, _, head = unit
            k_ref, _, size, key = piece
            cells = slice(sequence * size + key, sequence * size + key + part)
            return jnp.exp2(dot(k_ref[cells, channels(head, joined)], queries)).astype(BF16)

        queries = diagonal(units[0])
        weights = [weigh(units[0], queries, piece) for piece in pieces]
        for at, (sequence, start, head) in enumerate(units):
            following, total = [], None
            if at + 1 < len(units):
                queries = diagonal(units[at + 1])
            for piece, weight in zip(pieces, weights):
                if at + 1 < len(units):
                    following.append(weigh(units[at + 1], queries, piece))
                _, vt_ref, size, key = piece
                cells = slice(sequence * size + key, sequence * size + key + part)
                term = dot(with_ones(vt_ref, head, cells, part, joined), weight)
                total = term if total is None else total + term
            base = sequence * length + start
            queried = slice(base, base + tile)
            for own in range(joined):
                cols = slice(own * tile, (own + 1) * tile)
                share = total[channels(own), cols]
                norm = total[joined * WIDTH : joined * WIDTH + 8, cols]
                at_sum = (head + own) * STARTED
                at_norm = at_sum + WIDTH
                if unfinished:
                    att_ref[at_sum:at_norm, queried] = share
                    att_ref[at_norm : at_norm + 8, queried] = norm
                    continue
                if started is not None:
                    share = share + started[at_sum:at_norm, queried]
                    norm = norm + started[at_norm : at_norm + 8, queried]
                att_ref[channels(head + own), queried] = (share / norm[:1]).astype(BF16)
            weights = following

    if unfinished:
        fast()
        return
    pl.when(safe)(fast)

    @pl.when(jnp.logical_not(safe))
    def _():
        tiles = length // 256

        def step(t, carry):
            head = t % HEADS
            index = t // HEADS
            cols = pl.ds(pl.multiple_of(index * 256, 256), 256)
            rows = pl.ds(pl.multiple_of(head * WIDTH, WIDTH), WIDTH)
            owner = lax.broadcasted_iota(jnp.int32, (C, 256), 0) // WIDTH
            queries = jnp.where(owner == head, qt_ref[:, cols], jnp.zeros((C, 256), BF16))
            scores, owns = [], []
            for k_ref, _ in sources:
                size = k_ref.shape[0] // count
                owns.append(pl.ds(pl.multiple_of(index // tiles * size, size), size))
                scores.append(dot(k_ref[owns[-1], :], queries))
            tops = [jnp.max(score, axis=0, keepdims=True) for score in scores]
            top = functools.reduce(jnp.maximum, tops)
            mixed = 0.0
            for (_, vt_ref), score, own in zip(sources, scores, owns):
                expo = jnp.exp2(score - top).astype(BF16)
                ones = jnp.ones((16, score.shape[0]), BF16)
                mixed = mixed + dot(jnp.concatenate([vt_ref[rows, own], ones], axis=0), expo)
            att_ref[rows, cols] = (mixed[:WIDTH] / mixed[WIDTH : WIDTH + 1]).astype(BF16)
            return carry

        lax.fori_loop(0, count * tiles * HEADS, step, 0)


def row_kernel(
    edges, halo_rows, rows, wconv, bias, gain, wq_t, wk, wv_t, wout, out_ref,
    taps, hidden, normed, k_ref, qt_ref, vt_ref, att_ref, first,
):
    index = pl.program_id(0)
    length = hidden.shape[0]
    part = 256
    above = 2 * index if edges else 0
    if edges:
        at_rows = 3 * index, 1 + index
    else:
        at_rows = 1 + index, 2 + index

    def cells(ref, row, start):
        cols = ref.shape[2]
        return ref[start // cols : (start + part) // cols, row].reshape(part, C)

    flat = (length, C)
    taps[0:8, :] = jnp.zeros((8, 3 * C), F32)
    taps[length + 8 : length + 16, :] = jnp.zeros((8, 3 * C), F32)
    weights = jnp.concatenate([wconv[above], wconv[1], wconv[2 - above]], axis=0)
    for start in range(0, length, part):
        around = [cells(halo_rows, index, start)] + [cells(rows, row, start) for row in at_rows]
        total = dot(jnp.concatenate(around, axis=1), weights)
        taps[8 + start : 8 + start + part, :] = total
    for start in range(0, length, part):
        at = 8 + start
        pre = (
            taps[at - 1 : at - 1 + part, 0:C]
            + taps[at : at + part, C : 2 * C]
            + taps[at + 1 : at + 1 + part, 2 * C : 3 * C]
            + bias[...]
        )
        h = (cells(rows, at_rows[0], start).astype(F32) + jax.nn.gelu(pre)).astype(BF16)
        hidden[start : start + part, :] = h
        normed[start : start + part, :] = normalize(h.astype(F32), gain[...])
    rounded, q_square, k_square = project(normed[...], wq_t[...], wk[...], wv_t[...])
    k_ref[...], qt_ref[...], vt_ref[...] = rounded
    safe = q_square * k_square <= SAFE_SQUARE
    attend(safe, [(k_ref, vt_ref)], qt_ref, att_ref, 1, 512, 256, 1)
    result = hidden[...].astype(F32) + dot_tn(att_ref[...], wout[...])

    @pl.when(index == 0)
    def _():
        first[...] = result

    @pl.when(index == 1)
    def _():
        pair = [first[...].reshape(length // 8, 8, C), result.reshape(length // 8, 8, C)]
        out_ref[...] = jnp.concatenate(pair, axis=1).astype(BF16)


def whole(shape):
    return pl.BlockSpec(shape, lambda i: (0,) * len(shape))


def row_call(edges, halo, rows, wconv, bias, gain, wq_t, wk, wv_t, wout):
    devices, _, cols, _ = rows.shape
    length = devices * cols
    weights = [wconv, bias, gain, wq_t, wk, wv_t, wout]
    flops = 2 * length * C * (9 * C + 4 * C) * 2 + 2 * 2 * HEADS * length * length * 512
    return pl.pallas_call(
        functools.partial(row_kernel, edges),
        grid=(2,),
        in_specs=[pl.BlockSpec(memory_space=pltpu.VMEM)] * (2 + len(weights)),
        out_specs=whole((length // 8, 16, C)),
        out_shape=jax.ShapeDtypeStruct((length // 8, 16, C), BF16),
        scratch_shapes=[
            pltpu.VMEM((length + 16, 3 * C), F32),
            pltpu.VMEM((length, C), BF16),
            pltpu.VMEM((length, C), BF16),
            pltpu.VMEM((length, C), BF16),
            pltpu.VMEM((C, length), BF16),
            pltpu.VMEM((C, length), BF16),
            pltpu.VMEM((C, length), BF16),
            pltpu.VMEM((length, C), F32),
        ],
        cost_estimate=pl.CostEstimate(
            flops=flops, bytes_accessed=8 * length * C, transcendentals=2 * HEADS * length**2
        ),
        compiler_params=pltpu.CompilerParams(vmem_limit_bytes=36 * 2**20),
        name="edge_rows" if edges else "middle_rows",
    )(halo, rows, *weights)


def load_cells(block, left, right):
    cells = block[...].astype(F32).reshape(left.shape[0], C)
    left[...] = cells[:, :128]
    right[...] = cells[:, 128:]


def two_columns(index, length):
    return [pl.ds(2 * index + side, length, stride=8) for side in range(2)]


def project_columns(left, right, gain, wq_t, wk, wv_t, x_ref, k_ref, qt_ref, vt_ref, norms):
    index = pl.program_id(0)
    length = x_ref.shape[0] // 2
    columns = jnp.concatenate(
        [
            jnp.concatenate([left[cells, :], right[cells, :]], axis=1)
            for cells in two_columns(index, length)
        ],
        axis=0,
    )
    x_ref[...] = columns.astype(BF16)
    normed = normalize(columns, gain[...])
    rounded, q_square, k_square = project(normed, wq_t[...], wk[...], wv_t[...])
    k_ref[...], qt_ref[...], vt_ref[...] = rounded

    @pl.when(index == 0)
    def _():
        norms[...] = jnp.zeros(norms.shape, F32)

    norms[0] = jnp.maximum(norms[0], q_square)
    norms[1] = jnp.maximum(norms[1], k_square)


def attend_columns(
    norms, sources, qt_ref, x_ref, wout, att_ref, left, right, out_ref, started=None
):
    index = pl.program_id(0)
    length = x_ref.shape[0] // 2
    q_square, k_squares = jnp.max(norms[0][0]), [jnp.max(norm[1]) for norm in norms]
    safe = q_square * functools.reduce(jnp.maximum, k_squares) <= SAFE_SQUARE
    attend(safe, sources, qt_ref, att_ref, 2, 256, 256, 2, started)
    result = x_ref[...].astype(F32) + dot_tn(att_ref[...], wout[...])
    for side, cells in enumerate(two_columns(index, length)):
        left[cells, :] = result[side * length : (side + 1) * length, :128]
        right[cells, :] = result[side * length : (side + 1) * length, 128:]

    @pl.when(index == 3)
    def _():
        blocks, size, _ = out_ref.shape
        for half, ref in enumerate((left, right)):
            values = ref[...].reshape(size // 16, blocks, 16, 128)
            for block in range(blocks):
                part = values[:, block].reshape(size, 128)
                out_ref[block, :, 128 * half : 128 * half + 128] = part.astype(BF16)


def first_kernel(
    block, gain, wq_t, wk, wv_t, x_ref, k_ref, qt_ref, vt_ref, norms, sums, left, right
):
    @pl.when(pl.program_id(0) == 0)
    def _():
        load_cells(block, left, right)

    project_columns(left, right, gain, wq_t, wk, wv_t, x_ref, k_ref, qt_ref, vt_ref, norms)
    attend(None, [(k_ref, vt_ref)], qt_ref, sums, 2, 256, 256, 2, unfinished=True)


def second_kernel(
    block, gain, wq_t, wk, wv_t, wout, xa_ref, ka_ref, qta_ref, vta_ref, norms_a, sums,
    out_ref, x_ref, k_ref, qt_ref, vt_ref, norms, left, right, left_out, right_out, att_ref,
):
    @pl.when(pl.program_id(0) == 0)
    def _():
        load_cells(block, left, right)

    project_columns(left, right, gain, wq_t, wk, wv_t, x_ref, k_ref, qt_ref, vt_ref, norms)
    sources = [(ka_ref, vta_ref), (k_ref, vt_ref)]
    attend_columns(
        [norms_a, norms], sources, qta_ref, xa_ref, wout, att_ref, left_out, right_out, out_ref, sums
    )


def third_kernel(
    wout, ka_ref, vta_ref, norms_a, x_ref, k_ref, qt_ref, vt_ref, norms, out_ref,
    left, right, att_ref,
):
    sources = [(ka_ref, vta_ref), (k_ref, vt_ref)]
    attend_columns([norms, norms_a], sources, qt_ref, x_ref, wout, att_ref, left, right, out_ref)


def col_calls(gain, wq_t, wk, wv_t, wout, blocks):
    def calls(cells):
        pair = cells // 4
        spec_x = pl.BlockSpec((pair, C), lambda i: (i, 0))
        spec_t = pl.BlockSpec((C, pair), lambda i: (0, i))
        spec_n = whole((2, 8, 128))
        spec_s = pl.BlockSpec((HEADS * STARTED, pair), lambda i: (0, i))
        sums_shape = jax.ShapeDtypeStruct((HEADS * STARTED, cells), F32)
        part_specs = [spec_x, spec_x, spec_t, spec_t, spec_n]
        part_shapes = [
            jax.ShapeDtypeStruct((cells, C), BF16),
            jax.ShapeDtypeStruct((cells, C), BF16),
            jax.ShapeDtypeStruct((C, cells), BF16),
            jax.ShapeDtypeStruct((C, cells), BF16),
            jax.ShapeDtypeStruct((2, 8, 128), F32),
        ]
        out = (blocks, cells // blocks, C)
        out_shape = jax.ShapeDtypeStruct(out, BF16)
        halves = [pltpu.VMEM((cells, 128), F32)] * 2
        att = pltpu.VMEM((C, pair), BF16)
        project_flops = 2 * cells * C * 3 * C
        attend_flops = 2 * 2 * HEADS * cells * (cells // 4) * 256 + 2 * cells * C * C

        def call(kernel, name, args, in_specs, out_specs, out_shapes, scratch, flops, exps):
            return pl.pallas_call(
                kernel,
                grid=(4,),
                in_specs=in_specs,
                out_specs=out_specs,
                out_shape=out_shapes,
                scratch_shapes=scratch,
                cost_estimate=pl.CostEstimate(
                    flops=flops, bytes_accessed=8 * cells * C, transcendentals=exps
                ),
                compiler_params=pltpu.CompilerParams(vmem_limit_bytes=VMEM_LIMIT),
                name=name,
            )(*args)

        weights = [gain, wq_t, wk, wv_t]
        weight_specs = [whole(w.shape) for w in weights]
        wout_spec = whole(wout.shape)
        exps = HEADS * cells * cells // 4

        def first(block):
            return call(
                first_kernel, "first_projections", [block] + weights,
                [whole(block.shape)] + weight_specs, part_specs + [spec_s],
                part_shapes + [sums_shape], halves, project_flops + attend_flops // 2, exps // 2,
            )

        def second(block, part):
            results = call(
                second_kernel, "first_queries", [block] + weights + [wout] + list(part),
                [whole(block.shape)] + weight_specs + [wout_spec] + part_specs + [spec_s],
                [whole(out)] + part_specs, [out_shape] + part_shapes, halves * 2 + [att],
                project_flops + attend_flops // 2, exps // 2,
            )
            return results[0], results[1:]

        def third(part, other):
            return call(
                third_kernel, "second_queries",
                [wout, part[1], part[3], part[4]] + list(other),
                [wout_spec, spec_x, spec_t, spec_n] + part_specs, whole(out), out_shape,
                halves + [att], attend_flops, exps,
            )

        return first, second, third

    return calls


def split_weights(qkv):
    return qkv[:, :C].T, qkv[:, C : 2 * C], qkv[:, 2 * C :].T


def shards(
    radar_input, conv_weight, conv_bias, row_gain, row_qkv, row_out, col_gain, col_qkv, col_out
):
    gy, gx = lax.axis_size("gy"), lax.axis_size("gx")
    height, cols, _ = radar_input.shape
    wconv = conv_weight.transpose(0, 2, 1, 3).reshape(3, C, 3 * C)
    row_weights = (wconv, conv_bias.reshape(1, C), row_gain.reshape(1, C)) + split_weights(row_qkv)
    col_weights = (col_gain.reshape(1, C),) + split_weights(col_qkv)
    rows = radar_input.reshape(gx, height // gx, cols, C)
    rows = lax.all_to_all(rows, "gx", split_axis=0, concat_axis=0, tiled=True)
    count = gy * gx
    up = [(i, i + 1) for i in range(count - 1)]
    down = [(j, i) for i, j in up]
    above = lax.ppermute(rows[:, 3], ("gy", "gx"), up)
    below = lax.ppermute(rows[:, 0], ("gy", "gx"), down)
    middle = row_call(False, rows, rows, *row_weights, row_out)
    halo = jnp.stack([above, below], axis=1)
    edge = row_call(True, halo, rows, *row_weights, row_out)
    middle = lax.all_to_all(middle, ("gx", "gy"), split_axis=0, concat_axis=0, tiled=True)
    first, second, third = col_calls(*col_weights, col_out, gy)(middle.shape[0] * 16)
    part = first(middle)
    edge = lax.all_to_all(edge, ("gx", "gy"), split_axis=0, concat_axis=0, tiled=True)
    middle, other = second(edge, part)
    middle = lax.all_to_all(middle, "gy", split_axis=0, concat_axis=0, tiled=True)
    edge, middle = lax.optimization_barrier((third(part, other), middle))
    edge = lax.all_to_all(edge, "gy", split_axis=0, concat_axis=0, tiled=True)
    middle, edge = (
        rows.reshape(gy, height // 4, 2, cols // gy, C).transpose(1, 2, 0, 3, 4)
        for rows in (middle, edge)
    )
    result = jnp.concatenate([edge[:, :1], middle, edge[:, 1:]], axis=1)
    return result.reshape(height, cols, C)


def solution(mesh):
    in_specs = (P("gy", "gx", None), P(), P(), P(), P(), P(), P(), P(), P())
    out_specs = P("gy", "gx", None)
    return jax.shard_map(shards, mesh=mesh, in_specs=in_specs, out_specs=out_specs, check_vma=False)
```

profile of v0, /device:TPU:0, one launch (start us, length us, event | category | flops | bytes accessed | tf_op | source)
XLA Modules:
  0.0 294.8 jit_solution(11068296166495392526)
XLA Ops:
  0.0 0.0 copy-start.8
  0.0 7.2 %all-to-all-start = ((bf16[16,4,64,256]{3,2,1,0:T(8,128)(2,1)}), bf16[16,4,64,256]{3,2,1,0:T(8,128)(2,1)S(1)}, u32[]{:S(2)}, u32[]{:S(2)}) async-start(bf16[16,4,64,256]{3,2,1,0:T(8,128)(2,1)} %bitcast.37), calls=%async_computation | async-start | bytes 4194304 | tf_op jit(solution)/shard_map/all_to_all | solution.py:420
  7.3 1.8 fusion.2
  9.0 0.1 copy.29
  9.1 1.0 copy.28
  10.1 0.0 copy-done.8
  10.1 1.5 copy.18
  11.7 1.6 copy.21.wconv
  13.3 23.2 %all-to-all-done.halo_rows.rows = bf16[16,4,64,256]{3,2,1,0:T(8,128)(2,1)S(1)} async-done(((bf16[16,4,64,256]{3,2,1,0:T(8,128)(2,1)}), bf16[16,4,64,256]{3,2,1,0:T(8,128)(2,1)S(1)}, u32[]{:S(2)}, u32[]{:S(2)}) %all-to-all-start) | async-done | bytes 2097184 | tf_op jit(solution)/shard_map/all_to_all | solution.py:420
  36.5 1.1 slice_bitcast_fusion.1
  37.6 2.3 collective-permute-start
  39.9 1.3 collective-permute-start.1
  41.2 0.0 copy-done.6
  41.2 0.0 copy-done.7
  41.2 0.0 copy-done.2
  41.2 0.0 copy-done.4
  41.2 53.4 %middle_rows.1 = bf16[128,16,256]{2,1,0:T(8,128)(2,1)S(1)} custom-call(bf16[16,4,64,256]{3,2,1,0:T(8,128)(2,1)S(1)} %all-to-all-done.halo_rows.rows, bf16[16,4,64,256]{3,2,1,0:T(8,128)(2,1)S(1)} %all-to-all-done.halo_rows.rows, bf16[3,256,768]{2,1,0:T(8,128)(2,1)S(1)} %copy.21.wconv, f32[1,256]{1,0:T(1,128)S(1)} %bitcast.30, f32[1,256]{1,0:T(1,128)S(1)} %bitcast.32, ...), custom_call_target="tpu_custom_call" | custom-call | flops 20669530112 | bytes 2097152 | tf_op jit(solution)/shard_map/middle_rows/pallas_call | solution.py:221
  94.6 0.0 copy-start.1
  94.6 1.0 copy-done.1
  95.6 13.1 %all-to-all-start.1 = ((bf16[128,16,256]{2,1,0:T(8,128)(2,1)}), bf16[128,16,256]{2,1,0:T(8,128)(2,1)}, u32[]{:S(2)}, u32[]{:S(2)}) async-start(bf16[128,16,256]{2,1,0:T(8,128)(2,1)} %copy-done.1), calls=%async_computation.1 | async-start | bytes 2097152 | tf_op jit(solution)/shard_map/all_to_all | solution.py:429
  108.7 0.0 collective-permute-done
  108.7 0.0 collective-permute-done.1
  108.7 0.0 copy-start.3
  108.7 0.0 copy-start.5
  108.7 1.3 pad_maximum_fusion.1
  110.0 0.1 copy.25.halo_rows
  110.1 0.0 copy-done.3
  110.1 0.0 copy-done.5
  110.1 53.4 %edge_rows.1 = bf16[128,16,256]{2,1,0:T(8,128)(2,1)S(1)} custom-call(bf16[16,2,64,256]{3,2,1,0:T(8,128)(2,1)S(1)} %copy.25.halo_rows, bf16[16,4,64,256]{3,2,1,0:T(8,128)(2,1)S(1)} %all-to-all-done.halo_rows.rows, bf16[3,256,768]{2,1,0:T(8,128)(2,1)S(1)} %copy.21.wconv, f32[1,256]{1,0:T(1,128)S(1)} %bitcast.31, f32[1,256]{1,0:T(1,128)S(1)} %bitcast.33, ...), custom_call_target="tpu_custom_call" | custom-call | flops 20669530112 | bytes 2097152 | tf_op jit(solution)/shard_map/edge_rows/pallas_call | solution.py:221
  163.6 0.0 copy-start
  163.6 1.0 copy-done
  164.6 0.0 all-to-all-done.1.block
  164.6 9.7 %all-to-all-start.2 = ((bf16[128,16,256]{2,1,0:T(8,128)(2,1)}), bf16[128,16,256]{2,1,0:T(8,128)(2,1)S(1)}, u32[]{:S(2)}, u32[]{:S(2)}) async-start(bf16[128,16,256]{2,1,0:T(8,128)(2,1)} %copy-done), calls=%async_computation.2 | async-start | bytes 2097152 | tf_op jit(solution)/shard_map/all_to_all | solution.py:432
  174.3 0.0 copy-done.10
  174.3 0.7 fusion.1
  175.0 0.8 copy.31
  175.8 0.8 copy.30
  176.5 10.6 %first_projections.1 = (bf16[2048,256]{1,0:T(8,128)(2,1)}, bf16[2048,256]{1,0:T(8,128)(2,1)}, bf16[256,2048]{1,0:T(8,128)(2,1)}, bf16[256,2048]{1,0:T(8,128)(2,1...) custom-call(bf16[128,16,256]{2,1,0:T(8,128)(2,1)} %all-to-all-done.1.block, f32[1,256]{1,0:T(1,128)} %bitcast.42, ...), custom_call_target="tpu_custom_call" | custom-call | flops 5234491392 | bytes 4194304 | tf_op jit(solution)/shard_map/first_projections/pallas_call | solution.py:359
  187.1 6.4 %all-to-all-done.2.block = bf16[128,16,256]{2,1,0:T(8,128)(2,1)S(1)} async-done(((bf16[128,16,256]{2,1,0:T(8,128)(2,1)}), bf16[128,16,256]{2,1,0:T(8,128)(2,1)S(1)}, u32[]{:S(2)}, u32[]{:S(2)}) %all-to-all-start.2) | async-done | bytes 1048608 | tf_op jit(solution)/shard_map/all_to_all | solution.py:432
  193.5 1.0 copy-done.9
  194.4 39.3 %first_queries.1 = (bf16[8,256,256]{2,1,0:T(8,128)(2,1)}, bf16[2048,256]{1,0:T(8,128)(2,1)}, bf16[2048,256]{1,0:T(8,128)(2,1)}, bf16[256,2048]{1,0:T(8,128)(2,1)...) custom-call(bf16[128,16,256]{2,1,0:T(8,128)(2,1)} %copy-done.9, f32[1,256]{1,0:T(1,128)} %bitcast.43, ...), custom_call_target="tpu_custom_call" | custom-call | flops 5234491392 | bytes 4194304 | tf_op jit(solution)/shard_map/first_queries/pallas_call | solution.py:359
  233.7 3.6 %all-to-all-start.3 = ((bf16[8,256,256]{2,1,0:T(8,128)(2,1)}), bf16[8,256,256]{2,1,0:T(8,128)(2,1)S(1)}, u32[]{:S(2)}, u32[]{:S(2)}) async-start(bf16[8,256,256]{2,1,0:T(8,128)(2,1)} %get-tuple-element.30), calls=%async_computation.3 | async-start | bytes 2097152 | tf_op jit(solution)/shard_map/all_to_all | solution.py:434
  237.3 35.0 %second_queries.1 = bf16[8,256,256]{2,1,0:T(8,128)(2,1)} custom-call(bf16[256,256]{1,0:T(8,128)(2,1)} %wout.7, bf16[2048,256]{1,0:T(8,128)(2,1)} %get-tuple-element.19.ka_ref, bf16[256,2048]{1,0:T(8,128)(2,1)} %get-tuple-element.20.vta_ref, f32[2,8,128]{2,1,0:T(8,128)} %get-tuple-element.21.norms_a, bf16[2048,256]{1,0:T(8,128)(2,1)} %get-tuple-element.25.x_ref, ...), custom_call_target="tpu_custom_call" | custom-call | flops 8858370048 | bytes 4194304 | tf_op jit(solution)/shard_map/second_queries/pallas_call | solution.py:359
  272.3 0.0 all-to-all-done.3
  272.3 20.5 %all_to_all.25 = bf16[8,256,256]{2,1,0:T(8,128)(2,1)S(1)} all-to-all(bf16[8,256,256]{2,1,0:T(8,128)(2,1)} %second_queries.1), channel_id=1, replica_groups=mesh['gy'=8,'gx'=16] {'gy'}, dimensions={0} | all-to-all | bytes 2097152 | tf_op jit(solution)/shard_map/all_to_all | solution.py:436
  292.8 0.1 fusion
  292.9 0.2 pad_maximum_fusion
  293.2 1.6 copy.27
  (6 shorter events, 0.0 us)
Async XLA Ops:
  0.0 10.1 %copy-start.8 = (bf16[3,3,256,256]{3,2,1,0:T(8,128)(2,1)S(1)}, bf16[3,3,256,256]{3,2,1,0:T(8,128)(2,1)}, u32[]{:S(2)}) copy-start(bf16[3,3,256,256]{3,2,1,0:T(8,128)(2,1)} %param.10) | copy-start | bytes 3538948
  0.0 36.5 %all-to-all-start = ((bf16[16,4,64,256]{3,2,1,0:T(8,128)(2,1)}), bf16[16,4,64,256]{3,2,1,0:T(8,128)(2,1)S(1)}, u32[]{:S(2)}, u32[]{:S(2)}) async-start(bf16[16,4,64,256]{3,2,1,0:T(8,128)(2,1)} %bitcast.37), calls=%async_computation | async-start | bytes 4194304 | tf_op jit(solution)/shard_map/all_to_all | solution.py:420
  11.7 29.5 %copy-start.6 = (f32[256]{0:T(256)S(1)}, f32[256]{0:T(256)}, u32[]{:S(2)}) copy-start(f32[256]{0:T(256)} %param.11) | copy-start | bytes 3076
  11.7 29.5 %copy-start.7 = (f32[256]{0:T(256)S(1)}, f32[256]{0:T(256)}, u32[]{:S(2)}) copy-start(f32[256]{0:T(256)} %param.12) | copy-start | bytes 3076
  36.5 4.7 %copy-start.2 = (bf16[256,256]{1,0:T(8,128)(2,1)S(1)}, bf16[256,256]{1,0:T(8,128)(2,1)}, u32[]{:S(2)}) copy-start(bf16[256,256]{1,0:T(8,128)(2,1)} %get-tuple-element.42.wk) | copy-start | bytes 393220
  36.5 4.7 %copy-start.4 = (bf16[256,256]{1,0:T(8,128)(2,1)S(1)}, bf16[256,256]{1,0:T(8,128)(2,1)}, u32[]{:S(2)}) copy-start(bf16[256,256]{1,0:T(8,128)(2,1)} %wout.5) | copy-start | bytes 393220
  37.6 71.1 %collective-permute-start = (bf16[16,64,256]{2,1,0:T(8,128)(2,1)}, bf16[16,64,256]{2,1,0:T(8,128)(2,1)}, u32[]{:S(2)}, u32[]{:S(2)}) collective-permute-start(bf16[16,64,256]{2,1,0:T(8,128)(2,1)} %get-tuple-element.33), channel_id=1, source_target_pairs={{0,1},{1,2},{2,3},{3,4},{4,5},{5,6},{6,7},{7,8},{8,9},{9,10},{10,1... | collective-permute-start | bytes 1572872 | tf_op jit(solution)/shard_map/ppermute | solution.py:424
  39.9 68.8 %collective-permute-start.1 = (bf16[16,64,256]{2,1,0:T(8,128)(2,1)}, bf16[16,64,256]{2,1,0:T(8,128)(2,1)}, u32[]{:S(2)}, u32[]{:S(2)}) collective-permute-start(bf16[16,64,256]{2,1,0:T(8,128)(2,1)} %get-tuple-element.34), channel_id=1, source_target_pairs={{1,0},{2,1},{3,2},{4,3},{5,4},{6,5},{7,6},{8,7},{9,8},{10,9},{11,1... | collective-permute-start | bytes 1572872 | tf_op jit(solution)/shard_map/ppermute | solution.py:425
  94.6 1.0 copy-start.1
  95.6 69.0 %all-to-all-start.1 = ((bf16[128,16,256]{2,1,0:T(8,128)(2,1)}), bf16[128,16,256]{2,1,0:T(8,128)(2,1)}, u32[]{:S(2)}, u32[]{:S(2)}) async-start(bf16[128,16,256]{2,1,0:T(8,128)(2,1)} %copy-done.1), calls=%async_computation.1 | async-start | bytes 2097152 | tf_op jit(solution)/shard_map/all_to_all | solution.py:429
  108.7 1.4 copy-start.3
  108.7 1.4 copy-start.5
  163.6 1.0 copy-start
  164.6 9.8 %copy-start.10 = (bf16[256,768]{1,0:T(8,128)(2,1)S(1)}, bf16[256,768]{1,0:T(8,128)(2,1)}, u32[]{:S(2)}) copy-start(bf16[256,768]{1,0:T(8,128)(2,1)} %param.16) | copy-start | bytes 1179652
  164.6 28.9 %all-to-all-start.2 = ((bf16[128,16,256]{2,1,0:T(8,128)(2,1)}), bf16[128,16,256]{2,1,0:T(8,128)(2,1)S(1)}, u32[]{:S(2)}, u32[]{:S(2)}) async-start(bf16[128,16,256]{2,1,0:T(8,128)(2,1)} %copy-done), calls=%async_computation.2 | async-start | bytes 2097152 | tf_op jit(solution)/shard_map/all_to_all | solution.py:432
  193.5 1.0 copy-start.9
  233.7 38.6 %all-to-all-start.3 = ((bf16[8,256,256]{2,1,0:T(8,128)(2,1)}), bf16[8,256,256]{2,1,0:T(8,128)(2,1)S(1)}, u32[]{:S(2)}, u32[]{:S(2)}) async-start(bf16[8,256,256]{2,1,0:T(8,128)(2,1)} %get-tuple-element.30), calls=%async_computation.3 | async-start | bytes 2097152 | tf_op jit(solution)/shard_map/all_to_all | solution.py:434
where the time goes:
time: 295 us
  Pallas kernels  192 us (65%)
  starting transfers between devices  37.2 us (13%)
  waiting for transfers between devices  29.6 us (10%)
  blocking collectives  20.5 us (7%)
  local copies, waits for them, and re-layouts  14 us (5%)
    pallas_call x2, Pallas kernels, row_call(): pl.pallas_call(functools.partial(row_kernel, edges), grid=(2,), in_specs=...  107 us
    pallas_call x3, Pallas kernels, call(): pl.pallas_call(kernel, grid=(4,), in_specs=in_specs, out_specs=out_specs,...  84.9 us
    all_to_all x1, waiting for transfers between devices, shards(): rows = lax.all_to_all(rows, 'gx', split_axis=0, concat_axis=0, tiled=True)  23.2 us
    all_to_all x1, blocking collectives, shards(): edge = lax.all_to_all(edge, 'gy', split_axis=0, concat_axis=0, tiled=True)  20.5 us
    all_to_all x1, starting transfers between devices, shards(): lax.all_to_all(middle, ('gx', 'gy'), split_axis=0, concat_axis=0, tiled=T...  13.1 us
    all_to_all x1, starting transfers between devices, shards(): lax.all_to_all(edge, ('gx', 'gy'), split_axis=0, concat_axis=0, tiled=True)  9.74 us
    all_to_all x1, starting transfers between devices, shards(): rows = lax.all_to_all(rows, 'gx', split_axis=0, concat_axis=0, tiled=True)  7.25 us
    unnamed x27, local copies, waits for them, and re-layouts  7.09 us
  transfers between devices with their start and end apart: 6, of which 2 were waited for; matrix products, arithmetic and copies ran while one was open for 3% of the time, Pallas kernels for 52%

commit v1 on v0

--- a/solution.py
+++ b/solution.py
@@ -159,11 +159,11 @@
 
 def row_kernel(
     edges, halo_rows, rows, wconv, bias, gain, wq_t, wk, wv_t, wout, out_ref,
-    taps, hidden, normed, k_ref, qt_ref, vt_ref, att_ref, first,
+    taps, hidden, normed, k_ref, qt_ref, vt_ref, att_ref, first, both, sent,
 ):
     index = pl.program_id(0)
     length = hidden.shape[0]
-    part = 256
+    part = 128
     above = 2 * index if edges else 0
     if edges:
         at_rows = 3 * index, 1 + index
@@ -178,11 +178,15 @@
     taps[0:8, :] = jnp.zeros((8, 3 * C), F32)
     taps[length + 8 : length + 16, :] = jnp.zeros((8, 3 * C), F32)
     weights = jnp.concatenate([wconv[above], wconv[1], wconv[2 - above]], axis=0)
-    for start in range(0, length, part):
+    def convolve(start):
         around = [cells(halo_rows, index, start)] + [cells(rows, row, start) for row in at_rows]
         total = dot(jnp.concatenate(around, axis=1), weights)
         taps[8 + start : 8 + start + part, :] = total
+
+    convolve(0)
     for start in range(0, length, part):
+        if start + part < length:
+            convolve(start + part)
         at = 8 + start
         pre = (
             taps[at - 1 : at - 1 + part, 0:C]
@@ -206,7 +210,10 @@
     @pl.when(index == 1)
     def _():
         pair = [first[...].reshape(length // 8, 8, C), result.reshape(length // 8, 8, C)]
-        out_ref[...] = jnp.concatenate(pair, axis=1).astype(BF16)
+        both[...] = jnp.concatenate(pair, axis=1).astype(BF16)
+        copy = pltpu.make_async_copy(both, out_ref, sent)
+        copy.start()
+        copy.wait()
 
 
 def whole(shape):
@@ -222,7 +229,7 @@
         functools.partial(row_kernel, edges),
         grid=(2,),
         in_specs=[pl.BlockSpec(memory_space=pltpu.VMEM)] * (2 + len(weights)),
-        out_specs=whole((length // 8, 16, C)),
+        out_specs=pl.BlockSpec(memory_space=pltpu.HBM),
         out_shape=jax.ShapeDtypeStruct((length // 8, 16, C), BF16),
         scratch_shapes=[
             pltpu.VMEM((length + 16, 3 * C), F32),
@@ -233,6 +240,8 @@
             pltpu.VMEM((C, length), BF16),
             pltpu.VMEM((C, length), BF16),
             pltpu.VMEM((length, C), F32),
+            pltpu.VMEM((length // 8, 16, C), BF16),
+            pltpu.SemaphoreType.DMA,
         ],
         cost_estimate=pl.CostEstimate(
             flops=flops, bytes_accessed=8 * length * C, transcendentals=2 * HEADS * length**2
@@ -282,7 +291,7 @@
     length = x_ref.shape[0] // 2
     q_square, k_squares = jnp.max(norms[0][0]), [jnp.max(norm[1]) for norm in norms]
     safe = q_square * functools.reduce(jnp.maximum, k_squares) <= SAFE_SQUARE
-    attend(safe, sources, qt_ref, att_ref, 2, 256, 256, 2, started)
+    attend(safe, sources, qt_ref, att_ref, 2, 256, 256, 4, started)
     result = x_ref[...].astype(F32) + dot_tn(att_ref[...], wout[...])
     for side, cells in enumerate(two_columns(index, length)):
         left[cells, :] = result[side * length : (side + 1) * length, :128]
@@ -378,14 +387,14 @@
         def first(block):
             return call(
                 first_kernel, "first_projections", [block] + weights,
-                [whole(block.shape)] + weight_specs, part_specs + [spec_s],
+                [pl.BlockSpec(memory_space=pltpu.VMEM)] + weight_specs, part_specs + [spec_s],
                 part_shapes + [sums_shape], halves, project_flops + attend_flops // 2, exps // 2,
             )
 
         def second(block, part):
             results = call(
                 second_kernel, "first_queries", [block] + weights + [wout] + list(part),
-                [whole(block.shape)] + weight_specs + [wout_spec] + part_specs + [spec_s],
+                [pl.BlockSpec(memory_space=pltpu.VMEM)] + weight_specs + [wout_spec] + part_specs + [spec_s],
                 [whole(out)] + part_specs, [out_shape] + part_shapes, halves * 2 + [att],
                 project_flops + attend_flops // 2, exps // 2,
             )

time: 295 us -> 295 us (level)
  no operation moved by 1% of the time
where the time goes in v1:
time: 295 us; the launch traced here: 294 us
  Pallas kernels  191 us (65%)
  starting transfers between devices  37.2 us (13%)
  waiting for transfers between devices  29.6 us (10%)
  blocking collectives  20.5 us (7%)
  local copies, waits for them, and re-layouts  14 us (5%)
    pallas_call x2, Pallas kernels, row_call(): pl.pallas_call(functools.partial(row_kernel, edges), grid=(2,), in_specs=...  106 us
    pallas_call x3, Pallas kernels, call(): pl.pallas_call(kernel, grid=(4,), in_specs=in_specs, out_specs=out_specs,...  84.9 us
    all_to_all x1, waiting for transfers between devices, shards(): rows = lax.all_to_all(rows, 'gx', split_axis=0, concat_axis=0, tiled=True)  23.2 us
    all_to_all x1, blocking collectives, shards(): edge = lax.all_to_all(edge, 'gy', split_axis=0, concat_axis=0, tiled=True)  20.5 us
    all_to_all x1, starting transfers between devices, shards(): lax.all_to_all(middle, ('gx', 'gy'), split_axis=0, concat_axis=0, tiled=T...  13.1 us
    all_to_all x1, starting transfers between devices, shards(): lax.all_to_all(edge, ('gx', 'gy'), split_axis=0, concat_axis=0, tiled=True)  9.73 us
    all_to_all x1, starting transfers between devices, shards(): rows = lax.all_to_all(rows, 'gx', split_axis=0, concat_axis=0, tiled=True)  7.25 us
    unnamed x27, local copies, waits for them, and re-layouts  7.09 us
  transfers between devices with their start and end apart: 6, of which 2 were waited for; matrix products, arithmetic and copies ran while one was open for 3% of the time, Pallas kernels for 52%

profile of v1, /device:TPU:0, one launch (start us, length us, event | category | flops | bytes accessed | tf_op | source)
XLA Modules:
  0.0 294.3 jit_solution(14672400276099942080)
XLA Ops:
  0.0 0.0 copy-start.8
  0.0 7.2 %all-to-all-start = ((bf16[16,4,64,256]{3,2,1,0:T(8,128)(2,1)}), bf16[16,4,64,256]{3,2,1,0:T(8,128)(2,1)S(1)}, u32[]{:S(2)}, u32[]{:S(2)}) async-start(bf16[16,4,64,256]{3,2,1,0:T(8,128)(2,1)} %bitcast.37), calls=%async_computation | async-start | bytes 4194304 | tf_op jit(solution)/shard_map/all_to_all | solution.py:429
  7.3 1.8 fusion.2
  9.0 0.1 copy.29
  9.1 1.0 copy.28
  10.1 0.0 copy-done.8
  10.1 1.5 copy.18
  11.7 1.6 copy.21.wconv
  13.3 23.2 %all-to-all-done.halo_rows.rows = bf16[16,4,64,256]{3,2,1,0:T(8,128)(2,1)S(1)} async-done(((bf16[16,4,64,256]{3,2,1,0:T(8,128)(2,1)}), bf16[16,4,64,256]{3,2,1,0:T(8,128)(2,1)S(1)}, u32[]{:S(2)}, u32[]{:S(2)}) %all-to-all-start) | async-done | bytes 2097184 | tf_op jit(solution)/shard_map/all_to_all | solution.py:429
  36.5 1.1 slice_bitcast_fusion.1
  37.6 2.3 collective-permute-start
  39.9 1.3 collective-permute-start.1
  41.2 0.0 copy-done.6
  41.2 0.0 copy-done.7
  41.2 0.0 copy-done.2
  41.2 0.0 copy-done.4
  41.2 53.1 %middle_rows.1 = bf16[128,16,256]{2,1,0:T(8,128)(2,1)S(1)} custom-call(bf16[16,4,64,256]{3,2,1,0:T(8,128)(2,1)S(1)} %all-to-all-done.halo_rows.rows, bf16[16,4,64,256]{3,2,1,0:T(8,128)(2,1)S(1)} %all-to-all-done.halo_rows.rows, bf16[3,256,768]{2,1,0:T(8,128)(2,1)S(1)} %copy.21.wconv, f32[1,256]{1,0:T(1,128)S(1)} %bitcast.30, f32[1,256]{1,0:T(1,128)S(1)} %bitcast.32, ...), custom_call_target="tpu_custom_call" | custom-call | flops 20669530112 | bytes 2097152 | tf_op jit(solution)/shard_map/middle_rows/pallas_call | solution.py:228
  94.3 0.0 copy-start.1
  94.4 1.0 copy-done.1
  95.3 13.1 %all-to-all-start.1 = ((bf16[128,16,256]{2,1,0:T(8,128)(2,1)}), bf16[128,16,256]{2,1,0:T(8,128)(2,1)}, u32[]{:S(2)}, u32[]{:S(2)}) async-start(bf16[128,16,256]{2,1,0:T(8,128)(2,1)} %copy-done.1), calls=%async_computation.1 | async-start | bytes 2097152 | tf_op jit(solution)/shard_map/all_to_all | solution.py:438
  108.4 0.0 collective-permute-done
  108.4 0.0 collective-permute-done.1
  108.4 0.0 copy-start.3
  108.4 0.0 copy-start.5
  108.4 1.3 pad_maximum_fusion.1
  109.8 0.1 copy.25.halo_rows
  109.9 0.0 copy-done.3
  109.9 0.0 copy-done.5
  109.9 53.2 %edge_rows.1 = bf16[128,16,256]{2,1,0:T(8,128)(2,1)S(1)} custom-call(bf16[16,2,64,256]{3,2,1,0:T(8,128)(2,1)S(1)} %copy.25.halo_rows, bf16[16,4,64,256]{3,2,1,0:T(8,128)(2,1)S(1)} %all-to-all-done.halo_rows.rows, bf16[3,256,768]{2,1,0:T(8,128)(2,1)S(1)} %copy.21.wconv, f32[1,256]{1,0:T(1,128)S(1)} %bitcast.31, f32[1,256]{1,0:T(1,128)S(1)} %bitcast.33, ...), custom_call_target="tpu_custom_call" | custom-call | flops 20669530112 | bytes 2097152 | tf_op jit(solution)/shard_map/edge_rows/pallas_call | solution.py:228
  163.0 0.0 copy-start
  163.0 1.0 copy-done
  164.0 0.0 all-to-all-done.1.block
  164.0 9.7 %all-to-all-start.2 = ((bf16[128,16,256]{2,1,0:T(8,128)(2,1)}), bf16[128,16,256]{2,1,0:T(8,128)(2,1)S(1)}, u32[]{:S(2)}, u32[]{:S(2)}) async-start(bf16[128,16,256]{2,1,0:T(8,128)(2,1)} %copy-done), calls=%async_computation.2 | async-start | bytes 2097152 | tf_op jit(solution)/shard_map/all_to_all | solution.py:441
  173.8 0.0 copy-done.10
  173.8 0.7 fusion.1
  174.5 0.8 copy.31
  175.2 0.8 copy.30
  176.0 10.6 %first_projections.1 = (bf16[2048,256]{1,0:T(8,128)(2,1)}, bf16[2048,256]{1,0:T(8,128)(2,1)}, bf16[256,2048]{1,0:T(8,128)(2,1)}, bf16[256,2048]{1,0:T(8,128)(2,1...) custom-call(bf16[128,16,256]{2,1,0:T(8,128)(2,1)} %all-to-all-done.1.block, f32[1,256]{1,0:T(1,128)} %bitcast.42, ...), custom_call_target="tpu_custom_call" | custom-call | flops 5234491392 | bytes 4194304 | tf_op jit(solution)/shard_map/first_projections/pallas_call | solution.py:368
  186.6 6.4 %all-to-all-done.2.block = bf16[128,16,256]{2,1,0:T(8,128)(2,1)S(1)} async-done(((bf16[128,16,256]{2,1,0:T(8,128)(2,1)}), bf16[128,16,256]{2,1,0:T(8,128)(2,1)S(1)}, u32[]{:S(2)}, u32[]{:S(2)}) %all-to-all-start.2) | async-done | bytes 1048608 | tf_op jit(solution)/shard_map/all_to_all | solution.py:441
  192.9 1.0 copy-done.9
  193.9 39.3 %first_queries.1 = (bf16[8,256,256]{2,1,0:T(8,128)(2,1)}, bf16[2048,256]{1,0:T(8,128)(2,1)}, bf16[2048,256]{1,0:T(8,128)(2,1)}, bf16[256,2048]{1,0:T(8,128)(2,1)...) custom-call(bf16[128,16,256]{2,1,0:T(8,128)(2,1)} %copy-done.9, f32[1,256]{1,0:T(1,128)} %bitcast.43, ...), custom_call_target="tpu_custom_call" | custom-call | flops 5234491392 | bytes 4194304 | tf_op jit(solution)/shard_map/first_queries/pallas_call | solution.py:368
  233.2 3.6 %all-to-all-start.3 = ((bf16[8,256,256]{2,1,0:T(8,128)(2,1)}), bf16[8,256,256]{2,1,0:T(8,128)(2,1)S(1)}, u32[]{:S(2)}, u32[]{:S(2)}) async-start(bf16[8,256,256]{2,1,0:T(8,128)(2,1)} %get-tuple-element.30), calls=%async_computation.3 | async-start | bytes 2097152 | tf_op jit(solution)/shard_map/all_to_all | solution.py:443
  236.8 35.0 %second_queries.1 = bf16[8,256,256]{2,1,0:T(8,128)(2,1)} custom-call(bf16[256,256]{1,0:T(8,128)(2,1)} %wout.7, bf16[2048,256]{1,0:T(8,128)(2,1)} %get-tuple-element.19.ka_ref, bf16[256,2048]{1,0:T(8,128)(2,1)} %get-tuple-element.20.vta_ref, f32[2,8,128]{2,1,0:T(8,128)} %get-tuple-element.21.norms_a, bf16[2048,256]{1,0:T(8,128)(2,1)} %get-tuple-element.25.x_ref, ...), custom_call_target="tpu_custom_call" | custom-call | flops 8858370048 | bytes 4194304 | tf_op jit(solution)/shard_map/second_queries/pallas_call | solution.py:368
  271.8 0.0 all-to-all-done.3
  271.8 20.5 %all_to_all.25 = bf16[8,256,256]{2,1,0:T(8,128)(2,1)S(1)} all-to-all(bf16[8,256,256]{2,1,0:T(8,128)(2,1)} %second_queries.1), channel_id=1, replica_groups=mesh['gy'=8,'gx'=16] {'gy'}, dimensions={0} | all-to-all | bytes 2097152 | tf_op jit(solution)/shard_map/all_to_all | solution.py:445
  292.3 0.1 fusion
  292.4 0.2 pad_maximum_fusion
  292.7 1.6 copy.27
  (6 shorter events, 0.0 us)
Async XLA Ops:
  0.0 10.1 %copy-start.8 = (bf16[3,3,256,256]{3,2,1,0:T(8,128)(2,1)S(1)}, bf16[3,3,256,256]{3,2,1,0:T(8,128)(2,1)}, u32[]{:S(2)}) copy-start(bf16[3,3,256,256]{3,2,1,0:T(8,128)(2,1)} %param.10) | copy-start | bytes 3538948
  0.0 36.5 %all-to-all-start = ((bf16[16,4,64,256]{3,2,1,0:T(8,128)(2,1)}), bf16[16,4,64,256]{3,2,1,0:T(8,128)(2,1)S(1)}, u32[]{:S(2)}, u32[]{:S(2)}) async-start(bf16[16,4,64,256]{3,2,1,0:T(8,128)(2,1)} %bitcast.37), calls=%async_computation | async-start | bytes 4194304 | tf_op jit(solution)/shard_map/all_to_all | solution.py:429
  11.7 29.5 %copy-start.6 = (f32[256]{0:T(256)S(1)}, f32[256]{0:T(256)}, u32[]{:S(2)}) copy-start(f32[256]{0:T(256)} %param.11) | copy-start | bytes 3076
  11.7 29.5 %copy-start.7 = (f32[256]{0:T(256)S(1)}, f32[256]{0:T(256)}, u32[]{:S(2)}) copy-start(f32[256]{0:T(256)} %param.12) | copy-start | bytes 3076
  36.5 4.7 %copy-start.2 = (bf16[256,256]{1,0:T(8,128)(2,1)S(1)}, bf16[256,256]{1,0:T(8,128)(2,1)}, u32[]{:S(2)}) copy-start(bf16[256,256]{1,0:T(8,128)(2,1)} %get-tuple-element.42.wk) | copy-start | bytes 393220
  36.5 4.7 %copy-start.4 = (bf16[256,256]{1,0:T(8,128)(2,1)S(1)}, bf16[256,256]{1,0:T(8,128)(2,1)}, u32[]{:S(2)}) copy-start(bf16[256,256]{1,0:T(8,128)(2,1)} %wout.5) | copy-start | bytes 393220
  37.6 70.8 %collective-permute-start = (bf16[16,64,256]{2,1,0:T(8,128)(2,1)}, bf16[16,64,256]{2,1,0:T(8,128)(2,1)}, u32[]{:S(2)}, u32[]{:S(2)}) collective-permute-start(bf16[16,64,256]{2,1,0:T(8,128)(2,1)} %get-tuple-element.33), channel_id=1, source_target_pairs={{0,1},{1,2},{2,3},{3,4},{4,5},{5,6},{6,7},{7,8},{8,9},{9,10},{10,1... | collective-permute-start | bytes 1572872 | tf_op jit(solution)/shard_map/ppermute | solution.py:433
  39.9 68.5 %collective-permute-start.1 = (bf16[16,64,256]{2,1,0:T(8,128)(2,1)}, bf16[16,64,256]{2,1,0:T(8,128)(2,1)}, u32[]{:S(2)}, u32[]{:S(2)}) collective-permute-start(bf16[16,64,256]{2,1,0:T(8,128)(2,1)} %get-tuple-element.34), channel_id=1, source_target_pairs={{1,0},{2,1},{3,2},{4,3},{5,4},{6,5},{7,6},{8,7},{9,8},{10,9},{11,1... | collective-permute-start | bytes 1572872 | tf_op jit(solution)/shard_map/ppermute | solution.py:434
  94.3 1.0 copy-start.1
  95.3 68.7 %all-to-all-start.1 = ((bf16[128,16,256]{2,1,0:T(8,128)(2,1)}), bf16[128,16,256]{2,1,0:T(8,128)(2,1)}, u32[]{:S(2)}, u32[]{:S(2)}) async-start(bf16[128,16,256]{2,1,0:T(8,128)(2,1)} %copy-done.1), calls=%async_computation.1 | async-start | bytes 2097152 | tf_op jit(solution)/shard_map/all_to_all | solution.py:438
  108.4 1.4 copy-start.3
  108.4 1.4 copy-start.5
  163.0 1.0 copy-start
  164.0 9.7 %copy-start.10 = (bf16[256,768]{1,0:T(8,128)(2,1)S(1)}, bf16[256,768]{1,0:T(8,128)(2,1)}, u32[]{:S(2)}) copy-start(bf16[256,768]{1,0:T(8,128)(2,1)} %param.16) | copy-start | bytes 1179652
  164.0 28.9 %all-to-all-start.2 = ((bf16[128,16,256]{2,1,0:T(8,128)(2,1)}), bf16[128,16,256]{2,1,0:T(8,128)(2,1)S(1)}, u32[]{:S(2)}, u32[]{:S(2)}) async-start(bf16[128,16,256]{2,1,0:T(8,128)(2,1)} %copy-done), calls=%async_computation.2 | async-start | bytes 2097152 | tf_op jit(solution)/shard_map/all_to_all | solution.py:441
  192.9 1.0 copy-start.9
  233.2 38.6 %all-to-all-start.3 = ((bf16[8,256,256]{2,1,0:T(8,128)(2,1)}), bf16[8,256,256]{2,1,0:T(8,128)(2,1)S(1)}, u32[]{:S(2)}, u32[]{:S(2)}) async-start(bf16[8,256,256]{2,1,0:T(8,128)(2,1)} %get-tuple-element.30), calls=%async_computation.3 | async-start | bytes 2097152 | tf_op jit(solution)/shard_map/all_to_all | solution.py:443

commit v2 on v1

--- a/solution.py
+++ b/solution.py
@@ -120,7 +120,7 @@
                 if started is not None:
                     share = share + started[at_sum:at_norm, queried]
                     norm = norm + started[at_norm : at_norm + 8, queried]
-                att_ref[channels(head + own), queried] = (share / norm[:1]).astype(BF16)
+                att_ref[channels(head + own), queried] = (share * (1.0 / norm[:1])).astype(BF16)
             weights = following
 
     if unfinished:

time: 295 us -> 295 us (level)
  no operation moved by 1% of the time
where the time goes in v2:
time: 295 us; the launch traced here: 294 us
  Pallas kernels  191 us (65%)
  starting transfers between devices  37.2 us (13%)
  waiting for transfers between devices  29.6 us (10%)
  blocking collectives  20.5 us (7%)
  local copies, waits for them, and re-layouts  14 us (5%)
    pallas_call x2, Pallas kernels, row_call(): pl.pallas_call(functools.partial(row_kernel, edges), grid=(2,), in_specs=...  106 us
    pallas_call x3, Pallas kernels, call(): pl.pallas_call(kernel, grid=(4,), in_specs=in_specs, out_specs=out_specs,...  84.9 us
    all_to_all x1, waiting for transfers between devices, shards(): rows = lax.all_to_all(rows, 'gx', split_axis=0, concat_axis=0, tiled=True)  23.2 us
    all_to_all x1, blocking collectives, shards(): edge = lax.all_to_all(edge, 'gy', split_axis=0, concat_axis=0, tiled=True)  20.5 us
    all_to_all x1, starting transfers between devices, shards(): lax.all_to_all(middle, ('gx', 'gy'), split_axis=0, concat_axis=0, tiled=T...  13.1 us
    all_to_all x1, starting transfers between devices, shards(): lax.all_to_all(edge, ('gx', 'gy'), split_axis=0, concat_axis=0, tiled=True)  9.73 us
    all_to_all x1, starting transfers between devices, shards(): rows = lax.all_to_all(rows, 'gx', split_axis=0, concat_axis=0, tiled=True)  7.25 us
    unnamed x27, local copies, waits for them, and re-layouts  7.09 us
  transfers between devices with their start and end apart: 6, of which 2 were waited for; matrix products, arithmetic and copies ran while one was open for 3% of the time, Pallas kernels for 52%

profile of v2, /device:TPU:0, one launch (start us, length us, event | category | flops | bytes accessed | tf_op | source)
XLA Modules:
  0.0 294.3 jit_solution(9714089822372660314)
XLA Ops:
  0.0 0.0 copy-start.8
  0.0 7.2 %all-to-all-start = ((bf16[16,4,64,256]{3,2,1,0:T(8,128)(2,1)}), bf16[16,4,64,256]{3,2,1,0:T(8,128)(2,1)S(1)}, u32[]{:S(2)}, u32[]{:S(2)}) async-start(bf16[16,4,64,256]{3,2,1,0:T(8,128)(2,1)} %bitcast.37), calls=%async_computation | async-start | bytes 4194304 | tf_op jit(solution)/shard_map/all_to_all | solution.py:429
  7.3 1.8 fusion.2
  9.0 0.1 copy.29
  9.1 1.0 copy.28
  10.1 0.0 copy-done.8
  10.1 1.5 copy.18
  11.7 1.6 copy.21.wconv
  13.3 23.2 %all-to-all-done.halo_rows.rows = bf16[16,4,64,256]{3,2,1,0:T(8,128)(2,1)S(1)} async-done(((bf16[16,4,64,256]{3,2,1,0:T(8,128)(2,1)}), bf16[16,4,64,256]{3,2,1,0:T(8,128)(2,1)S(1)}, u32[]{:S(2)}, u32[]{:S(2)}) %all-to-all-start) | async-done | bytes 2097184 | tf_op jit(solution)/shard_map/all_to_all | solution.py:429
  36.5 1.1 slice_bitcast_fusion.1
  37.6 2.3 collective-permute-start
  39.9 1.3 collective-permute-start.1
  41.2 0.0 copy-done.6
  41.2 0.0 copy-done.7
  41.2 0.0 copy-done.2
  41.2 0.0 copy-done.4
  41.2 53.1 %middle_rows.1 = bf16[128,16,256]{2,1,0:T(8,128)(2,1)S(1)} custom-call(bf16[16,4,64,256]{3,2,1,0:T(8,128)(2,1)S(1)} %all-to-all-done.halo_rows.rows, bf16[16,4,64,256]{3,2,1,0:T(8,128)(2,1)S(1)} %all-to-all-done.halo_rows.rows, bf16[3,256,768]{2,1,0:T(8,128)(2,1)S(1)} %copy.21.wconv, f32[1,256]{1,0:T(1,128)S(1)} %bitcast.30, f32[1,256]{1,0:T(1,128)S(1)} %bitcast.32, ...), custom_call_target="tpu_custom_call" | custom-call | flops 20669530112 | bytes 2097152 | tf_op jit(solution)/shard_map/middle_rows/pallas_call | solution.py:228
  94.3 0.0 copy-start.1
  94.4 1.0 copy-done.1
  95.3 13.1 %all-to-all-start.1 = ((bf16[128,16,256]{2,1,0:T(8,128)(2,1)}), bf16[128,16,256]{2,1,0:T(8,128)(2,1)}, u32[]{:S(2)}, u32[]{:S(2)}) async-start(bf16[128,16,256]{2,1,0:T(8,128)(2,1)} %copy-done.1), calls=%async_computation.1 | async-start | bytes 2097152 | tf_op jit(solution)/shard_map/all_to_all | solution.py:438
  108.4 0.0 collective-permute-done
  108.4 0.0 collective-permute-done.1
  108.4 0.0 copy-start.3
  108.4 0.0 copy-start.5
  108.4 1.3 pad_maximum_fusion.1
  109.8 0.1 copy.25.halo_rows
  109.9 0.0 copy-done.3
  109.9 0.0 copy-done.5
  109.9 53.2 %edge_rows.1 = bf16[128,16,256]{2,1,0:T(8,128)(2,1)S(1)} custom-call(bf16[16,2,64,256]{3,2,1,0:T(8,128)(2,1)S(1)} %copy.25.halo_rows, bf16[16,4,64,256]{3,2,1,0:T(8,128)(2,1)S(1)} %all-to-all-done.halo_rows.rows, bf16[3,256,768]{2,1,0:T(8,128)(2,1)S(1)} %copy.21.wconv, f32[1,256]{1,0:T(1,128)S(1)} %bitcast.31, f32[1,256]{1,0:T(1,128)S(1)} %bitcast.33, ...), custom_call_target="tpu_custom_call" | custom-call | flops 20669530112 | bytes 2097152 | tf_op jit(solution)/shard_map/edge_rows/pallas_call | solution.py:228
  163.0 0.0 copy-start
  163.0 1.0 copy-done
  164.0 0.0 all-to-all-done.1.block
  164.0 9.7 %all-to-all-start.2 = ((bf16[128,16,256]{2,1,0:T(8,128)(2,1)}), bf16[128,16,256]{2,1,0:T(8,128)(2,1)S(1)}, u32[]{:S(2)}, u32[]{:S(2)}) async-start(bf16[128,16,256]{2,1,0:T(8,128)(2,1)} %copy-done), calls=%async_computation.2 | async-start | bytes 2097152 | tf_op jit(solution)/shard_map/all_to_all | solution.py:441
  173.8 0.0 copy-done.10
  173.8 0.7 fusion.1
  174.5 0.8 copy.31
  175.2 0.8 copy.30
  176.0 10.6 %first_projections.1 = (bf16[2048,256]{1,0:T(8,128)(2,1)}, bf16[2048,256]{1,0:T(8,128)(2,1)}, bf16[256,2048]{1,0:T(8,128)(2,1)}, bf16[256,2048]{1,0:T(8,128)(2,1...) custom-call(bf16[128,16,256]{2,1,0:T(8,128)(2,1)} %all-to-all-done.1.block, f32[1,256]{1,0:T(1,128)} %bitcast.42, ...), custom_call_target="tpu_custom_call" | custom-call | flops 5234491392 | bytes 4194304 | tf_op jit(solution)/shard_map/first_projections/pallas_call | solution.py:368
  186.6 6.4 %all-to-all-done.2.block = bf16[128,16,256]{2,1,0:T(8,128)(2,1)S(1)} async-done(((bf16[128,16,256]{2,1,0:T(8,128)(2,1)}), bf16[128,16,256]{2,1,0:T(8,128)(2,1)S(1)}, u32[]{:S(2)}, u32[]{:S(2)}) %all-to-all-start.2) | async-done | bytes 1048608 | tf_op jit(solution)/shard_map/all_to_all | solution.py:441
  192.9 1.0 copy-done.9
  193.9 39.3 %first_queries.1 = (bf16[8,256,256]{2,1,0:T(8,128)(2,1)}, bf16[2048,256]{1,0:T(8,128)(2,1)}, bf16[2048,256]{1,0:T(8,128)(2,1)}, bf16[256,2048]{1,0:T(8,128)(2,1)...) custom-call(bf16[128,16,256]{2,1,0:T(8,128)(2,1)} %copy-done.9, f32[1,256]{1,0:T(1,128)} %bitcast.43, ...), custom_call_target="tpu_custom_call" | custom-call | flops 5234491392 | bytes 4194304 | tf_op jit(solution)/shard_map/first_queries/pallas_call | solution.py:368
  233.2 3.6 %all-to-all-start.3 = ((bf16[8,256,256]{2,1,0:T(8,128)(2,1)}), bf16[8,256,256]{2,1,0:T(8,128)(2,1)S(1)}, u32[]{:S(2)}, u32[]{:S(2)}) async-start(bf16[8,256,256]{2,1,0:T(8,128)(2,1)} %get-tuple-element.30), calls=%async_computation.3 | async-start | bytes 2097152 | tf_op jit(solution)/shard_map/all_to_all | solution.py:443
  236.8 35.0 %second_queries.1 = bf16[8,256,256]{2,1,0:T(8,128)(2,1)} custom-call(bf16[256,256]{1,0:T(8,128)(2,1)} %wout.7, bf16[2048,256]{1,0:T(8,128)(2,1)} %get-tuple-element.19.ka_ref, bf16[256,2048]{1,0:T(8,128)(2,1)} %get-tuple-element.20.vta_ref, f32[2,8,128]{2,1,0:T(8,128)} %get-tuple-element.21.norms_a, bf16[2048,256]{1,0:T(8,128)(2,1)} %get-tuple-element.25.x_ref, ...), custom_call_target="tpu_custom_call" | custom-call | flops 8858370048 | bytes 4194304 | tf_op jit(solution)/shard_map/second_queries/pallas_call | solution.py:368
  271.8 0.0 all-to-all-done.3
  271.8 20.5 %all_to_all.25 = bf16[8,256,256]{2,1,0:T(8,128)(2,1)S(1)} all-to-all(bf16[8,256,256]{2,1,0:T(8,128)(2,1)} %second_queries.1), channel_id=1, replica_groups=mesh['gy'=8,'gx'=16] {'gy'}, dimensions={0} | all-to-all | bytes 2097152 | tf_op jit(solution)/shard_map/all_to_all | solution.py:445
  292.3 0.1 fusion
  292.4 0.2 pad_maximum_fusion
  292.7 1.6 copy.27
  (6 shorter events, 0.0 us)
Async XLA Ops:
  0.0 10.1 %copy-start.8 = (bf16[3,3,256,256]{3,2,1,0:T(8,128)(2,1)S(1)}, bf16[3,3,256,256]{3,2,1,0:T(8,128)(2,1)}, u32[]{:S(2)}) copy-start(bf16[3,3,256,256]{3,2,1,0:T(8,128)(2,1)} %param.10) | copy-start | bytes 3538948
  0.0 36.5 %all-to-all-start = ((bf16[16,4,64,256]{3,2,1,0:T(8,128)(2,1)}), bf16[16,4,64,256]{3,2,1,0:T(8,128)(2,1)S(1)}, u32[]{:S(2)}, u32[]{:S(2)}) async-start(bf16[16,4,64,256]{3,2,1,0:T(8,128)(2,1)} %bitcast.37), calls=%async_computation | async-start | bytes 4194304 | tf_op jit(solution)/shard_map/all_to_all | solution.py:429
  11.7 29.5 %copy-start.6 = (f32[256]{0:T(256)S(1)}, f32[256]{0:T(256)}, u32[]{:S(2)}) copy-start(f32[256]{0:T(256)} %param.11) | copy-start | bytes 3076
  11.7 29.5 %copy-start.7 = (f32[256]{0:T(256)S(1)}, f32[256]{0:T(256)}, u32[]{:S(2)}) copy-start(f32[256]{0:T(256)} %param.12) | copy-start | bytes 3076
  36.5 4.7 %copy-start.2 = (bf16[256,256]{1,0:T(8,128)(2,1)S(1)}, bf16[256,256]{1,0:T(8,128)(2,1)}, u32[]{:S(2)}) copy-start(bf16[256,256]{1,0:T(8,128)(2,1)} %get-tuple-element.42.wk) | copy-start | bytes 393220
  36.5 4.7 %copy-start.4 = (bf16[256,256]{1,0:T(8,128)(2,1)S(1)}, bf16[256,256]{1,0:T(8,128)(2,1)}, u32[]{:S(2)}) copy-start(bf16[256,256]{1,0:T(8,128)(2,1)} %wout.5) | copy-start | bytes 393220
  37.6 70.8 %collective-permute-start = (bf16[16,64,256]{2,1,0:T(8,128)(2,1)}, bf16[16,64,256]{2,1,0:T(8,128)(2,1)}, u32[]{:S(2)}, u32[]{:S(2)}) collective-permute-start(bf16[16,64,256]{2,1,0:T(8,128)(2,1)} %get-tuple-element.33), channel_id=1, source_target_pairs={{0,1},{1,2},{2,3},{3,4},{4,5},{5,6},{6,7},{7,8},{8,9},{9,10},{10,1... | collective-permute-start | bytes 1572872 | tf_op jit(solution)/shard_map/ppermute | solution.py:433
  39.9 68.5 %collective-permute-start.1 = (bf16[16,64,256]{2,1,0:T(8,128)(2,1)}, bf16[16,64,256]{2,1,0:T(8,128)(2,1)}, u32[]{:S(2)}, u32[]{:S(2)}) collective-permute-start(bf16[16,64,256]{2,1,0:T(8,128)(2,1)} %get-tuple-element.34), channel_id=1, source_target_pairs={{1,0},{2,1},{3,2},{4,3},{5,4},{6,5},{7,6},{8,7},{9,8},{10,9},{11,1... | collective-permute-start | bytes 1572872 | tf_op jit(solution)/shard_map/ppermute | solution.py:434
  94.3 1.0 copy-start.1
  95.3 68.7 %all-to-all-start.1 = ((bf16[128,16,256]{2,1,0:T(8,128)(2,1)}), bf16[128,16,256]{2,1,0:T(8,128)(2,1)}, u32[]{:S(2)}, u32[]{:S(2)}) async-start(bf16[128,16,256]{2,1,0:T(8,128)(2,1)} %copy-done.1), calls=%async_computation.1 | async-start | bytes 2097152 | tf_op jit(solution)/shard_map/all_to_all | solution.py:438
  108.4 1.4 copy-start.3
  108.4 1.4 copy-start.5
  163.0 1.0 copy-start
  164.0 9.7 %copy-start.10 = (bf16[256,768]{1,0:T(8,128)(2,1)S(1)}, bf16[256,768]{1,0:T(8,128)(2,1)}, u32[]{:S(2)}) copy-start(bf16[256,768]{1,0:T(8,128)(2,1)} %param.16) | copy-start | bytes 1179652
  164.0 28.9 %all-to-all-start.2 = ((bf16[128,16,256]{2,1,0:T(8,128)(2,1)}), bf16[128,16,256]{2,1,0:T(8,128)(2,1)S(1)}, u32[]{:S(2)}, u32[]{:S(2)}) async-start(bf16[128,16,256]{2,1,0:T(8,128)(2,1)} %copy-done), calls=%async_computation.2 | async-start | bytes 2097152 | tf_op jit(solution)/shard_map/all_to_all | solution.py:441
  192.9 1.0 copy-start.9
  233.2 38.6 %all-to-all-start.3 = ((bf16[8,256,256]{2,1,0:T(8,128)(2,1)}), bf16[8,256,256]{2,1,0:T(8,128)(2,1)S(1)}, u32[]{:S(2)}, u32[]{:S(2)}) async-start(bf16[8,256,256]{2,1,0:T(8,128)(2,1)} %get-tuple-element.30), calls=%async_computation.3 | async-start | bytes 2097152 | tf_op jit(solution)/shard_map/all_to_all | solution.py:443
